TPU v7x, 256 devices: a whole 4x4x8 slice. The times are simulated.
256 devices in a mesh: row: 8 (over x, y_hi), col: 16 (over y_lo, z), layer: 2 (over core).
Axes of the slice: x: 4, y: 4 (y_hi: 2, y_lo: 2; y = y_hi * 2 + y_lo), z: 8, core: 2. Of those that a mesh axis runs over, the one named last changes fastest.
Arguments:
- upper: float32 [1536, 7, 128, 128], P(('row', 'col')), may hold values from -2.5 to 2.5
- block_mask: int32 [1536, 7], P(('row', 'col')), may hold values 0 or 1
- keep_mask: int32 [1536, 13], P(('row', 'col')), may hold values 0 or 1
Outputs:
- product: float32 [1536, 13, 128, 128], P(('row', 'col'), None, 'layer')
All inputs are finite; a program needn't handle non-finite values. No bound on the sum of `block_mask` or of `keep_mask` on one device may be relied on, other than what follows from the above.
Results may differ from a plain program's by a relative error of at most 0.0001.
Values sent between devices are 32-bit elements; how exact they have to be, the bound alone decides.
A program may use at most 128 MiB of HBM per device.

v0:
```python
import functools

import jax
import jax.numpy as jnp
from jax import lax
from jax.experimental import pallas as pl
from jax.experimental.pallas import tpu as pltpu
from jax.sharding import PartitionSpec as P

MESH = pl.DeviceIdType.MESH
B = 128
H = 6
ROWS = 12
PAIRS = ROWS // 2
WINDOW = 2 * H + 2
HALF = B // 2


def masked(weight, block):
    return block * weight


def split(x):
    hi = x.astype(jnp.bfloat16)
    lo = (x - hi.astype(jnp.float32)).astype(jnp.bfloat16)
    return hi, lo


def kernel(
    up, mask_s, mask_v, keep_s, out,
    own, behind, ahead, mask_b, mask_a, right_hi, right_lo, left,
    load_sem, send_sem, recv_sem, pass_send, pass_recv, mask_send, mask_recv, ready,
):
    row, col, layer = lax.axis_index("row"), lax.axis_index("col"), lax.axis_index("layer")
    n_col = lax.axis_size("col")
    n_part = lax.axis_size("row") * n_col
    total_rows = n_part * ROWS
    part = row * n_col + col
    after = lax.rem(part + 1, n_part)
    before = lax.rem(part + n_part - 1, n_part)
    nxt = (after // n_col, lax.rem(after, n_col), layer)
    prv = (before // n_col, lax.rem(before, n_col), layer)
    sib = (row, col, 1 - layer)
    first_row = part * ROWS
    half = pl.ds(pl.multiple_of(layer * HALF, HALF), HALF)

    def head(j):
        return pltpu.make_async_remote_copy(
            src_ref=up.at[j, :, half, :], dst_ref=ahead.at[j, :, half, :],
            send_sem=send_sem.at[j], recv_sem=recv_sem.at[j], device_id=prv, device_id_type=MESH)

    def tail(a):
        return pltpu.make_async_remote_copy(
            src_ref=up.at[ROWS - 1 - a, pl.ds(a + 1, H - a), half, :],
            dst_ref=behind.at[a, pl.ds(0, H - a), half, :],
            send_sem=send_sem.at[H + a], recv_sem=recv_sem.at[H + a], device_id=nxt, device_id_type=MESH)

    def head_pass(j):
        return pltpu.make_async_remote_copy(
            src_ref=ahead.at[j, :, half, :], dst_ref=ahead.at[j, :, half, :],
            send_sem=pass_send.at[j], recv_sem=pass_recv.at[j], device_id=sib, device_id_type=MESH)

    def tail_pass(a):
        return pltpu.make_async_remote_copy(
            src_ref=behind.at[a, pl.ds(0, H - a), half, :], dst_ref=behind.at[a, pl.ds(0, H - a), half, :],
            send_sem=pass_send.at[H + a], recv_sem=pass_recv.at[H + a], device_id=sib, device_id_type=MESH)

    mask_head = pltpu.make_async_remote_copy(
        src_ref=mask_v, dst_ref=mask_a, send_sem=mask_send.at[0], recv_sem=mask_recv.at[0],
        device_id=prv, device_id_type=MESH)
    mask_tail = pltpu.make_async_remote_copy(
        src_ref=mask_v, dst_ref=mask_b, send_sem=mask_send.at[1], recv_sem=mask_recv.at[1],
        device_id=nxt, device_id_type=MESH)
    load = pltpu.make_async_copy(up, own, load_sem)

    barrier = pltpu.get_barrier_semaphore()
    pl.semaphore_signal(barrier, inc=1, device_id=nxt, device_id_type=MESH)
    pl.semaphore_signal(barrier, inc=1, device_id=sib, device_id_type=MESH)
    load.start()
    pl.semaphore_wait(barrier, 2)
    mask_head.start()
    for j in range(H):
        head(j).start()
    pl.semaphore_signal(ready, inc=1, device_id=prv, device_id_type=MESH)

    zero_right = jnp.zeros((B, B), jnp.bfloat16)
    zero_left = jnp.zeros((HALF, B), jnp.bfloat16)

    def clear(pair, carry):
        for ref in (right_hi, right_lo):
            ref[pair, pl.ds(0, B), pl.ds(B, B)] = zero_right
            ref[pair, pl.ds((WINDOW - 1) * B, B), pl.ds(0, B)] = zero_right
        return carry

    lax.fori_loop(0, 2 * PAIRS, clear, 0)

    def clear_left(pair, carry):
        for base in (0, B):
            left[pair, pl.ds(base, HALF), pl.ds((WINDOW - 1) * B, B)] = zero_left
            left[pair, pl.ds(base + HALF, HALF), pl.ds(0, B)] = zero_left
        return carry

    lax.fori_loop(0, PAIRS, clear_left, 0)

    pl.semaphore_wait(ready, 1)
    mask_tail.start()
    for a in range(H):
        tail(a).start()
    load.wait()

    def place_right(pair, r, k, x):
        hi, lo = split(x)
        at = pair + (r + k) // 2
        rows = pl.ds((r + H - 2 * ((r + k) // 2)) * B, B)
        lanes = pl.ds(((r + k) % 2) * B, B)
        right_hi[at, rows, lanes] = hi
        right_lo[at, rows, lanes] = lo

    def place_right_t(pair, r, k, xt):
        hi, lo = split(xt)
        rows = pl.ds((r + k + H) * B, B)
        right_hi[pair, rows, pl.ds(r * B, B)] = hi
        right_lo[pair, rows, pl.ds(r * B, B)] = lo

    def my_half(x):
        return jnp.where(layer == 0, x[:HALF], x[HALF:])

    def place_left(pair, r, offset, xh):
        hi, lo = split(xh)
        lanes = pl.ds((r + offset + H) * B, B)
        left[pair, pl.ds(r * HALF, HALF), lanes] = hi
        left[pair, pl.ds(B + r * HALF, HALF), lanes] = lo

    def own_pair(pair, carry):
        for r in range(2):
            for k in range(H + 1):
                j = 2 * pair + r
                inside = first_row + j + k < total_rows
                if k > 0:
                    inside = inside & (mask_s[j, k] == 1)
                weight = jnp.where(inside, jnp.float32(1.0), jnp.float32(0.0))
                x = masked(weight, own[j, k])
                xt = x.T
                if k == 0:
                    x = 0.5 * (x + xt)
                place_right(pair, r, k, x)
                place_left(pair, r, k, my_half(x))
                if k > 0:
                    place_right_t(pair, r, k, xt)
                    own_row = pair + (r + k) // 2

                    @pl.when(own_row < PAIRS)
                    def _():
                        place_left(own_row, (r + k) % 2, -k, my_half(xt))

        return carry

    lax.fori_loop(0, PAIRS, own_pair, 0)

    def multiply(pair, d, lo_block, hi_block):
        n = (hi_block - lo_block) * B
        lanes = pl.ds((2 * d + lo_block) * B, n)
        rows = pl.ds(lo_block * B, n)
        both = jnp.dot(left[pair, :, lanes], right_hi[pair + d, rows, :], preferred_element_type=jnp.float32)
        rest = jnp.dot(left[pair, pl.ds(0, B), lanes], right_lo[pair + d, rows, :], preferred_element_type=jnp.float32)
        return both[:B] + (both[B:] + rest)

    def emit(pair, d, total, add):
        for r in range(2):
            for s in range(2):
                m = 2 * d + s - r
                if 0 <= m <= 2 * H:
                    i = 2 * pair + r
                    kept = (keep_s[i, m] == 1) & (first_row + i + m < total_rows)
                    weight = jnp.where(kept, jnp.float32(1.0), jnp.float32(0.0))
                    piece = total[r * HALF : (r + 1) * HALF, s * B : (s + 1) * B] * weight
                    if add:
                        out[i, m] += piece
                    else:
                        out[i, m] = piece

    def own_low(d, first):
        def body(pair, carry):
            emit(pair, d, multiply(pair, d, 0, WINDOW - 2 * d), False)
            return carry

        lax.fori_loop(first, H // 2, body, 0)

    for d in range(H + 1):
        own_low(d, max(0, H // 2 - d))
    for pair in range(H // 2, PAIRS):
        for d in range(H + 1):
            c = pair + d
            if c < PAIRS:
                emit(pair, d, multiply(pair, d, 0, WINDOW - 2 * d), False)
            elif c < PAIRS + H // 2:
                emit(pair, d, multiply(pair, d, 0, 2 * (PAIRS + H // 2 - c)), False)

    for a in range(H):
        tail(a).wait_recv()
        tail_pass(a).start()
    mask_tail.wait_recv()
    for a in range(H):
        tail_pass(a).wait_recv()
        j = -1 - a
        pair, r = j // 2, j % 2
        for k in range(a + 1, H + 1):
            present = (mask_b[pl.ds(ROWS + j, 1), pl.ds(k, 1)] == 1) & (part > 0)
            x = masked(jnp.where(present, jnp.float32(1.0), jnp.float32(0.0)), behind[a, k - a - 1])
            place_right(pair, r, k, x)
            place_left(pair + (r + k) // 2, (r + k) % 2, -k, my_half(x.T))
    for pair in range(H // 2):
        for d in range(H // 2 - pair):
            emit(pair, d, multiply(pair, d, 0, WINDOW - 2 * d), False)

    mask_head.wait_recv()
    for q in range(H // 2):
        for r in range(2):
            head(2 * q + r).wait_recv()
            head_pass(2 * q + r).start()
        for r in range(2):
            j = 2 * q + r
            head_pass(j).wait_recv()
            for k in range(H + 1):
                present = first_row + ROWS + j + k < total_rows
                weight = jnp.where(present, jnp.float32(1.0), jnp.float32(0.0))
                if k > 0:
                    weight = jnp.where(mask_a[pl.ds(j, 1), pl.ds(k, 1)] == 1, weight, jnp.float32(0.0))
                x = masked(weight, ahead[j, k])
                if k == 0:
                    x = 0.5 * (x + x.T)
                place_right(PAIRS + q, r, k, x)
                if 0 < k < H - j:
                    place_right_t(PAIRS + q, r, k, x.T)
        for pair in range(H // 2 + q, PAIRS):
            for c in range(PAIRS, PAIRS + q + H // 2 + 1):
                d = c - pair
                at = 2 * (PAIRS + q - (c - H // 2))
                first = c >= PAIRS + H // 2 and q == c - PAIRS - H // 2
                emit(pair, d, multiply(pair, d, at, at + 2), not first)

    for j in range(H):
        head(j).wait_send()
        tail(j).wait_send()
        head_pass(j).wait_send()
        tail_pass(j).wait_send()
    mask_head.wait_send()
    mask_tail.wait_send()


def on_device(upper, block_mask, keep_mask):
    f32, bf16 = jnp.float32, jnp.bfloat16
    window = WINDOW * B
    return pl.pallas_call(
        kernel,
        out_shape=jax.ShapeDtypeStruct((ROWS, 2 * H + 1, HALF, B), f32),
        in_specs=[
            pl.BlockSpec(memory_space=pltpu.HBM),
            pl.BlockSpec(memory_space=pltpu.SMEM),
            pl.BlockSpec(memory_space=pltpu.VMEM),
            pl.BlockSpec(memory_space=pltpu.SMEM),
        ],
        out_specs=pl.BlockSpec(memory_space=pltpu.VMEM),
        scratch_shapes=[
            pltpu.VMEM((ROWS, H + 1, B, B), f32),
            pltpu.VMEM((H, H, B, B), f32),
            pltpu.VMEM((H, H + 1, B, B), f32),
            pltpu.VMEM(block_mask.shape, jnp.int32),
            pltpu.VMEM(block_mask.shape, jnp.int32),
            pltpu.VMEM((2 * PAIRS, window, 2 * B), bf16),
            pltpu.VMEM((2 * PAIRS, window, 2 * B), bf16),
            pltpu.VMEM((PAIRS, 2 * B, window), bf16),
            pltpu.SemaphoreType.DMA,
            pltpu.SemaphoreType.DMA((2 * H,)),
            pltpu.SemaphoreType.DMA((2 * H,)),
            pltpu.SemaphoreType.DMA((2 * H,)),
            pltpu.SemaphoreType.DMA((2 * H,)),
            pltpu.SemaphoreType.DMA((2,)),
            pltpu.SemaphoreType.DMA((2,)),
            pltpu.SemaphoreType.REGULAR,
        ],
        compiler_params=pltpu.CompilerParams(
            collective_id=0, has_side_effects=True, vmem_limit_bytes=56 * 2**20
        ),
    )(upper, block_mask, block_mask, keep_mask)


def solution(mesh):
    in_specs = (
        P(("row", "col"), None, None, None),
        P(("row", "col"), None),
        P(("row", "col"), None),
    )
    out_specs = P(("row", "col"), None, "layer", None)
    return jax.shard_map(
        on_device, mesh=mesh, in_specs=in_specs, out_specs=out_specs, check_vma=False
    )
```

profile of v0, /device:TPU:1, one launch (start us, length us, event | category | flops | bytes accessed | tf_op | source)
XLA Modules:
  0.0 56.0 jit_solution(2643663790595831911)
XLA Ops:
  0.0 1.4 %copy.4.mask_s.mask_v = s32[12,7]{1,0:T(8,128)} copy(s32[12,7]{0,1:T(8,128)} %param.4) | data formatting | bytes 672 | tf_op args[1]
  1.4 49.0 %shard_map.37 = f32[12,13,64,128]{3,2,1,0:T(8,128)} custom-call(f32[12,7,128,128]{3,2,1,0:T(8,128)} %up.1, s32[12,7]{1,0:T(8,128)} %copy.4.mask_s.mask_v, s32[12,7]{1,0:T(8,128)} %copy.4.mask_s.mask_v, s32[12,13]{1,0:T(8,128)} %keep_s.1), custom_call_target="tpu_custom_call" | custom-call | tf_op jit(solution)/shard_map/pallas_call | solution.py:254
  50.4 5.6 %copy.7 = f32[12,13,64,128]{3,2,1,0:T(8,128)} copy(f32[12,13,64,128]{3,2,1,0:T(8,128)} %shard_map.37) | data formatting | bytes 10223616
where the time goes:
time: 56.2 us; the launch traced here: 56 us
  Pallas kernels  49 us (87%)
  local copies, waits for them, and re-layouts  6.95 us (12%)
    pallas_call x1, Pallas kernels, on_device(): pl.pallas_call(kernel, out_shape=jax.ShapeDtypeStruct((ROWS, 2 * H + 1, H...  49 us
    unnamed x2, local copies, waits for them, and re-layouts  6.95 us

commit v1 on v0

--- a/solution.py
+++ b/solution.py
@@ -26,9 +26,59 @@
     return hi, lo
 
 
+def window_product(left, right_hi, right_lo, pair, d, lo_block, hi_block):
+    n = (hi_block - lo_block) * B
+    lanes = pl.ds((2 * d + lo_block) * B, n)
+    rows = pl.ds(lo_block * B, n)
+    both = jnp.dot(left[pair, :, lanes], right_hi[pair + d, rows, :], preferred_element_type=jnp.float32)
+    rest = jnp.dot(left[pair, pl.ds(0, B), lanes], right_lo[pair + d, rows, :], preferred_element_type=jnp.float32)
+    return both[:B] + (both[B:] + rest)
+
+
+def places(d):
+    spots = [(r, s, 2 * d + s - r) for r in range(2) for s in range(2)]
+    return [spot for spot in spots if 0 <= spot[2] <= 2 * H]
+
+
+def quarter(total, r, s):
+    return total[r * HALF : (r + 1) * HALF, s * B : (s + 1) * B]
+
+
+def keep_weight(keep_s, i, m, first_row, total_rows):
+    kept = (keep_s[i, m] == 1) & (first_row + i + m < total_rows)
+    return jnp.where(kept, jnp.float32(1.0), jnp.float32(0.0))
+
+
+def finish(out, right_hi, right_lo, left, keep_s, final, tail, sem):
+    n_part = lax.axis_size("row") * lax.axis_size("col")
+    first_row = (lax.axis_index("row") * lax.axis_size("col") + lax.axis_index("col")) * ROWS
+    last = PAIRS - 1
+    done = ROWS - 2
+    copies = [pltpu.make_async_copy(out.at[pl.ds(2 * p, 2)], final.at[pl.ds(2 * p, 2)], sem.at[p]) for p in range(last)]
+    copies.append(pltpu.make_async_copy(out.at[done, pl.ds(0, 2)], final.at[done, pl.ds(0, 2)], sem.at[last]))
+    copies.append(pltpu.make_async_copy(out.at[done + 1, pl.ds(0, 1)], final.at[done + 1, pl.ds(0, 1)], sem.at[last + 1]))
+    for copy in copies:
+        copy.start()
+    for d in range(1, H + 1):
+        at = WINDOW - 2 * d - 2
+        total = window_product(left, right_hi, right_lo, last, d, at, at + 2)
+        for r, s, m in places(d):
+            piece = quarter(total, r, s) * keep_weight(keep_s, done + r, m, first_row, n_part * ROWS)
+            tail[r, m] = piece if d == H else out[done + r, m] + piece
+    n = 2 * H + 1
+    more = [
+        pltpu.make_async_copy(tail.at[0, pl.ds(2, n - 2)], final.at[done, pl.ds(2, n - 2)], sem.at[last + 2]),
+        pltpu.make_async_copy(tail.at[1, pl.ds(1, n - 1)], final.at[done + 1, pl.ds(1, n - 1)], sem.at[last + 3]),
+    ]
+    for copy in more:
+        copy.start()
+    for copy in copies + more:
+        copy.wait()
+
+
 def kernel(
-    up, mask_s, mask_v, keep_s, out,
-    own, behind, ahead, mask_b, mask_a, right_hi, right_lo, left,
+    up, mask_s, mask_v, keep_s, out, right_hi, right_lo, left,
+    own, behind, ahead, mask_b, mask_a,
     load_sem, send_sem, recv_sem, pass_send, pass_recv, mask_send, mask_recv, ready,
 ):
     row, col, layer = lax.axis_index("row"), lax.axis_index("col"), lax.axis_index("layer")
@@ -102,10 +152,6 @@
 
     lax.fori_loop(0, PAIRS, clear_left, 0)
 
-    pl.semaphore_wait(ready, 1)
-    mask_tail.start()
-    for a in range(H):
-        tail(a).start()
     load.wait()
 
     def place_right(pair, r, k, x):
@@ -137,7 +183,7 @@
                 j = 2 * pair + r
                 inside = first_row + j + k < total_rows
                 if k > 0:
-                    inside = inside & (mask_s[j, k] == 1)
+                    inside = inside & (mask_s[k, j] == 1)
                 weight = jnp.where(inside, jnp.float32(1.0), jnp.float32(0.0))
                 x = masked(weight, own[j, k])
                 xt = x.T
@@ -156,28 +202,22 @@
         return carry
 
     lax.fori_loop(0, PAIRS, own_pair, 0)
+    pl.semaphore_wait(ready, 1)
+    mask_tail.start()
+    for a in range(H):
+        tail(a).start()
 
     def multiply(pair, d, lo_block, hi_block):
-        n = (hi_block - lo_block) * B
-        lanes = pl.ds((2 * d + lo_block) * B, n)
-        rows = pl.ds(lo_block * B, n)
-        both = jnp.dot(left[pair, :, lanes], right_hi[pair + d, rows, :], preferred_element_type=jnp.float32)
-        rest = jnp.dot(left[pair, pl.ds(0, B), lanes], right_lo[pair + d, rows, :], preferred_element_type=jnp.float32)
-        return both[:B] + (both[B:] + rest)
+        return window_product(left, right_hi, right_lo, pair, d, lo_block, hi_block)
 
     def emit(pair, d, total, add):
-        for r in range(2):
-            for s in range(2):
-                m = 2 * d + s - r
-                if 0 <= m <= 2 * H:
-                    i = 2 * pair + r
-                    kept = (keep_s[i, m] == 1) & (first_row + i + m < total_rows)
-                    weight = jnp.where(kept, jnp.float32(1.0), jnp.float32(0.0))
-                    piece = total[r * HALF : (r + 1) * HALF, s * B : (s + 1) * B] * weight
-                    if add:
-                        out[i, m] += piece
-                    else:
-                        out[i, m] = piece
+        for r, s, m in places(d):
+            i = 2 * pair + r
+            piece = quarter(total, r, s) * keep_weight(keep_s, i, m, first_row, total_rows)
+            if add:
+                out[i, m] += piece
+            else:
+                out[i, m] = piece
 
     def own_low(d, first):
         def body(pair, carry):
@@ -205,7 +245,7 @@
         j = -1 - a
         pair, r = j // 2, j % 2
         for k in range(a + 1, H + 1):
-            present = (mask_b[pl.ds(ROWS + j, 1), pl.ds(k, 1)] == 1) & (part > 0)
+            present = (mask_b[pl.ds(k, 1), pl.ds(ROWS + j, 1)] == 1) & (part > 0)
             x = masked(jnp.where(present, jnp.float32(1.0), jnp.float32(0.0)), behind[a, k - a - 1])
             place_right(pair, r, k, x)
             place_left(pair + (r + k) // 2, (r + k) % 2, -k, my_half(x.T))
@@ -216,22 +256,23 @@
     mask_head.wait_recv()
     for q in range(H // 2):
         for r in range(2):
-            head(2 * q + r).wait_recv()
-            head_pass(2 * q + r).start()
-        for r in range(2):
             j = 2 * q + r
+            head(j).wait_recv()
+            head_pass(j).start()
             head_pass(j).wait_recv()
             for k in range(H + 1):
                 present = first_row + ROWS + j + k < total_rows
                 weight = jnp.where(present, jnp.float32(1.0), jnp.float32(0.0))
                 if k > 0:
-                    weight = jnp.where(mask_a[pl.ds(j, 1), pl.ds(k, 1)] == 1, weight, jnp.float32(0.0))
+                    weight = jnp.where(mask_a[pl.ds(k, 1), pl.ds(j, 1)] == 1, weight, jnp.float32(0.0))
                 x = masked(weight, ahead[j, k])
                 if k == 0:
                     x = 0.5 * (x + x.T)
                 place_right(PAIRS + q, r, k, x)
                 if 0 < k < H - j:
                     place_right_t(PAIRS + q, r, k, x.T)
+        if q == H // 2 - 1:
+            break
         for pair in range(H // 2 + q, PAIRS):
             for c in range(PAIRS, PAIRS + q + H // 2 + 1):
                 d = c - pair
@@ -251,25 +292,27 @@
 def on_device(upper, block_mask, keep_mask):
     f32, bf16 = jnp.float32, jnp.bfloat16
     window = WINDOW * B
-    return pl.pallas_call(
+    spread = pl.pallas_call(
         kernel,
-        out_shape=jax.ShapeDtypeStruct((ROWS, 2 * H + 1, HALF, B), f32),
+        out_shape=(
+            pltpu.VMEM((ROWS, 2 * H + 1, HALF, B), f32),
+            pltpu.VMEM((2 * PAIRS, window, 2 * B), bf16),
+            pltpu.VMEM((2 * PAIRS, window, 2 * B), bf16),
+            pltpu.VMEM((PAIRS, 2 * B, window), bf16),
+        ),
         in_specs=[
             pl.BlockSpec(memory_space=pltpu.HBM),
             pl.BlockSpec(memory_space=pltpu.SMEM),
             pl.BlockSpec(memory_space=pltpu.VMEM),
             pl.BlockSpec(memory_space=pltpu.SMEM),
         ],
-        out_specs=pl.BlockSpec(memory_space=pltpu.VMEM),
+        out_specs=[pl.BlockSpec(memory_space=pltpu.VMEM)] * 4,
         scratch_shapes=[
             pltpu.VMEM((ROWS, H + 1, B, B), f32),
             pltpu.VMEM((H, H, B, B), f32),
             pltpu.VMEM((H, H + 1, B, B), f32),
-            pltpu.VMEM(block_mask.shape, jnp.int32),
-            pltpu.VMEM(block_mask.shape, jnp.int32),
-            pltpu.VMEM((2 * PAIRS, window, 2 * B), bf16),
-            pltpu.VMEM((2 * PAIRS, window, 2 * B), bf16),
-            pltpu.VMEM((PAIRS, 2 * B, window), bf16),
+            pltpu.VMEM((H + 1, ROWS), jnp.int32),
+            pltpu.VMEM((H + 1, ROWS), jnp.int32),
             pltpu.SemaphoreType.DMA,
             pltpu.SemaphoreType.DMA((2 * H,)),
             pltpu.SemaphoreType.DMA((2 * H,)),
@@ -280,9 +323,23 @@
             pltpu.SemaphoreType.REGULAR,
         ],
         compiler_params=pltpu.CompilerParams(
-            collective_id=0, has_side_effects=True, vmem_limit_bytes=56 * 2**20
+            collective_id=0, has_side_effects=True, vmem_limit_bytes=18 * 2**20
         ),
-    )(upper, block_mask, block_mask, keep_mask)
+    )
+    masks = block_mask.T
+    parts = spread(upper, masks, masks, keep_mask)
+    parts = [pltpu.with_memory_space_constraint(x, pltpu.VMEM) for x in parts]
+    return pl.pallas_call(
+        finish,
+        out_shape=jax.ShapeDtypeStruct((ROWS, 2 * H + 1, HALF, B), f32),
+        in_specs=[pl.BlockSpec(memory_space=pltpu.VMEM)] * 4 + [pl.BlockSpec(memory_space=pltpu.SMEM)],
+        out_specs=pl.BlockSpec(memory_space=pltpu.HBM),
+        scratch_shapes=[
+            pltpu.VMEM((2, 2 * H + 1, HALF, B), f32),
+            pltpu.SemaphoreType.DMA((PAIRS + 3,)),
+        ],
+        compiler_params=pltpu.CompilerParams(vmem_limit_bytes=8 * 2**20),
+    )(*parts, keep_mask)
 
 
 def solution(mesh):

time: 56.2 us -> 57.6 us (1.025)
  Pallas kernels: 49 us -> 56 us
  local copies, waits for them, and re-layouts: 6.95 us -> 1.38 us
    pallas_call x1 -> x2, Pallas kernels: 49 us -> 56 us  [the longest x1 52.9 us: on_device(): parts = spread(upper, masks, masks, keep_mask)]
    unnamed x2 -> x4, local copies, waits for them, and re-layouts: 6.95 us -> 1.38 us
where the time goes in v1:
time: 57.6 us; the launch traced here: 57.4 us
  Pallas kernels  56 us (97%)
  local copies, waits for them, and re-layouts  1.38 us (2%)
    pallas_call x1, Pallas kernels, on_device(): parts = spread(upper, masks, masks, keep_mask)  52.9 us
    pallas_call x1, Pallas kernels, on_device(): pl.pallas_call(finish, out_shape=jax.ShapeDtypeStruct((ROWS, 2 * H + 1, H...  3.1 us
    unnamed x4, local copies, waits for them, and re-layouts  1.38 us

profile of v1, /device:TPU:1, one launch (start us, length us, event | category | flops | bytes accessed | tf_op | source)
XLA Modules:
  0.0 57.4 jit_solution(3631137816873333161)
XLA Ops:
  0.0 0.0 copy-start
  0.0 0.7 %copy-done = s32[12,13]{1,0:T(8,128)S(1)} copy-done((s32[12,13]{1,0:T(8,128)S(1)}, s32[12,13]{1,0:T(8,128)}, u32[]{:S(2)}) %copy-start) | copy-done | bytes 648
  0.7 0.0 copy-start.1
  0.7 0.7 %copy-done.1 = s32[12,7]{0,1:T(8,128)S(1)} copy-done((s32[12,7]{0,1:T(8,128)S(1)}, s32[12,7]{0,1:T(8,128)}, u32[]{:S(2)}) %copy-start.1) | copy-done | bytes 360
  1.4 52.9 %shard_map.37 = (f32[12,13,64,128]{3,2,1,0:T(8,128)S(1)}, bf16[12,1792,256]{2,1,0:T(8,128)(2,1)S(1)}, bf16[12,1792,256]{2,1,0:T(8,128)(2,1)S(1)}, bf16[6,256,1792]{2,1,0:T(8,128)(2,1)S(1)}) custom-call(f32[12,7,128,128]{3,2,1,0:T(8,128)} %up.1, s32[7,12]{1,0:T(8,128)S(1)} %bitcast.1, s32[7,12]{1,0:T(8,128)S(1)} %bitcast.2, s32[12,13]{1,0:T(8,128)S(1)} %copy-done), custom_call_target="tpu_custom_call" | custom-call | tf_op jit(solution)/shard_map/pallas_call | solution.py:330
  54.3 3.1 %shard_map.38 = f32[12,13,64,128]{3,2,1,0:T(8,128)} custom-call(f32[12,13,64,128]{3,2,1,0:T(8,128)S(1)} %get-tuple-element.9.out, bf16[12,1792,256]{2,1,0:T(8,128)(2,1)S(1)} %get-tuple-element.10.right_hi, bf16[12,1792,256]{2,1,0:T(8,128)(2,1)S(1)} %get-tuple-element.11.right_lo, bf16[6,256,1792]{2,1,0:T(8,128)(2,1)S(1)} %get-tuple-element.12.left, ...), custom_call_target="tpu_custom_call" | custom-call | tf_op jit(solution)/shard_map/pallas_call | solution.py:332
Async XLA Ops:
  0.0 0.7 %copy-start = (s32[12,13]{1,0:T(8,128)S(1)}, s32[12,13]{1,0:T(8,128)}, u32[]{:S(2)}) copy-start(s32[12,13]{1,0:T(8,128)} %keep_s.3) | copy-start | bytes 1876
  0.7 0.7 %copy-start.1 = (s32[12,7]{0,1:T(8,128)S(1)}, s32[12,7]{0,1:T(8,128)}, u32[]{:S(2)}) copy-start(s32[12,7]{0,1:T(8,128)} %param.4) | copy-start | bytes 1012

commit v2 on v1

--- a/solution.py
+++ b/solution.py
@@ -77,8 +77,8 @@
 
 
 def kernel(
-    up, mask_s, mask_v, keep_s, out, right_hi, right_lo, left,
-    own, behind, ahead, mask_b, mask_a,
+    up, mask, keep, out, right_hi, right_lo, left,
+    own, behind, ahead, mask_b, mask_a, mask_s, keep_s, raw, folded, corner, folded_a, corner_a,
     load_sem, send_sem, recv_sem, pass_send, pass_recv, mask_send, mask_recv, ready,
 ):
     row, col, layer = lax.axis_index("row"), lax.axis_index("col"), lax.axis_index("layer")
@@ -96,7 +96,7 @@
 
     def head(j):
         return pltpu.make_async_remote_copy(
-            src_ref=up.at[j, :, half, :], dst_ref=ahead.at[j, :, half, :],
+            src_ref=up.at[j, pl.ds(1, H), half, :], dst_ref=ahead.at[j, :, half, :],
             send_sem=send_sem.at[j], recv_sem=recv_sem.at[j], device_id=prv, device_id_type=MESH)
 
     def tail(a):
@@ -116,22 +116,53 @@
             send_sem=pass_send.at[H + a], recv_sem=pass_recv.at[H + a], device_id=sib, device_id_type=MESH)
 
     mask_head = pltpu.make_async_remote_copy(
-        src_ref=mask_v, dst_ref=mask_a, send_sem=mask_send.at[0], recv_sem=mask_recv.at[0],
+        src_ref=mask, dst_ref=mask_a, send_sem=mask_send.at[0], recv_sem=mask_recv.at[0],
         device_id=prv, device_id_type=MESH)
     mask_tail = pltpu.make_async_remote_copy(
-        src_ref=mask_v, dst_ref=mask_b, send_sem=mask_send.at[1], recv_sem=mask_recv.at[1],
+        src_ref=mask, dst_ref=mask_b, send_sem=mask_send.at[1], recv_sem=mask_recv.at[1],
         device_id=nxt, device_id_type=MESH)
-    load = pltpu.make_async_copy(up, own, load_sem)
+    fold_half = pl.ds(pl.multiple_of(layer * (HALF // 2), HALF // 2), HALF // 2)
+    fold_send = pltpu.make_async_remote_copy(
+        src_ref=folded.at[:, fold_half, :], dst_ref=folded_a.at[:, fold_half, :],
+        send_sem=mask_send.at[2], recv_sem=mask_recv.at[2], device_id=prv, device_id_type=MESH)
+    fold_pass = pltpu.make_async_remote_copy(
+        src_ref=folded_a.at[:, fold_half, :], dst_ref=folded_a.at[:, fold_half, :],
+        send_sem=mask_send.at[3], recv_sem=mask_recv.at[3], device_id=sib, device_id_type=MESH)
+    corner_send = pltpu.make_async_remote_copy(
+        src_ref=corner, dst_ref=corner_a, send_sem=mask_send.at[4], recv_sem=mask_recv.at[4],
+        device_id=prv, device_id_type=MESH)
+    load_diagonal = pltpu.make_async_copy(up.at[pl.ds(0, H), 0], raw, load_sem.at[0])
+    load = pltpu.make_async_copy(up, own, load_sem.at[1])
+    load_mask = pltpu.make_async_copy(mask, mask_s, load_sem.at[2])
+    load_keep = pltpu.make_async_copy(keep, keep_s, load_sem.at[3])
 
     barrier = pltpu.get_barrier_semaphore()
     pl.semaphore_signal(barrier, inc=1, device_id=nxt, device_id_type=MESH)
     pl.semaphore_signal(barrier, inc=1, device_id=sib, device_id_type=MESH)
+    load_diagonal.start()
+    load_mask.start()
+    load_keep.start()
     load.start()
     pl.semaphore_wait(barrier, 2)
     mask_head.start()
-    for j in range(H):
+    for j in range(H - 2):
         head(j).start()
     pl.semaphore_signal(ready, inc=1, device_id=prv, device_id_type=MESH)
+
+    load_diagonal.wait()
+    row_at = lax.broadcasted_iota(jnp.int32, (HALF, B), 0)
+    lane_at = lax.broadcasted_iota(jnp.int32, (HALF, B), 1)
+    corner[...] = jnp.zeros_like(corner)
+    for j in range(H):
+        x = raw[j]
+        x = 0.5 * (x + x.T)
+        low = x[HALF:]
+        folded[j] = jnp.where(lane_at < row_at, pltpu.roll(low, HALF, 1), x[:HALF])
+        corner[pl.ds(j, 1), :] = jnp.sum(jnp.where(lane_at == row_at + HALF, low, 0.0), axis=0, keepdims=True)
+    fold_send.start()
+    corner_send.start()
+    for j in range(H - 2, H):
+        head(j).start()
 
     zero_right = jnp.zeros((B, B), jnp.bfloat16)
     zero_left = jnp.zeros((HALF, B), jnp.bfloat16)
@@ -152,6 +183,12 @@
 
     lax.fori_loop(0, PAIRS, clear_left, 0)
 
+    pl.semaphore_wait(ready, 1)
+    mask_tail.start()
+    for a in range(H):
+        tail(a).start()
+    load_mask.wait()
+    load_keep.wait()
     load.wait()
 
     def place_right(pair, r, k, x):
@@ -202,10 +239,6 @@
         return carry
 
     lax.fori_loop(0, PAIRS, own_pair, 0)
-    pl.semaphore_wait(ready, 1)
-    mask_tail.start()
-    for a in range(H):
-        tail(a).start()
 
     def multiply(pair, d, lo_block, hi_block):
         return window_product(left, right_hi, right_lo, pair, d, lo_block, hi_block)
@@ -239,6 +272,9 @@
     for a in range(H):
         tail(a).wait_recv()
         tail_pass(a).start()
+    for j in range(2):
+        head(j).wait_recv()
+        head_pass(j).start()
     mask_tail.wait_recv()
     for a in range(H):
         tail_pass(a).wait_recv()
@@ -254,25 +290,36 @@
             emit(pair, d, multiply(pair, d, 0, WINDOW - 2 * d), False)
 
     mask_head.wait_recv()
-    for q in range(H // 2):
-        for r in range(2):
-            j = 2 * q + r
-            head(j).wait_recv()
-            head_pass(j).start()
-            head_pass(j).wait_recv()
-            for k in range(H + 1):
-                present = first_row + ROWS + j + k < total_rows
-                weight = jnp.where(present, jnp.float32(1.0), jnp.float32(0.0))
-                if k > 0:
-                    weight = jnp.where(mask_a[pl.ds(k, 1), pl.ds(j, 1)] == 1, weight, jnp.float32(0.0))
-                x = masked(weight, ahead[j, k])
-                if k == 0:
-                    x = 0.5 * (x + x.T)
-                place_right(PAIRS + q, r, k, x)
-                if 0 < k < H - j:
-                    place_right_t(PAIRS + q, r, k, x.T)
-        if q == H // 2 - 1:
-            break
+    corner_send.wait_recv()
+    row_at = lax.broadcasted_iota(jnp.int32, (B, B), 0)
+    lane_at = lax.broadcasted_iota(jnp.int32, (B, B), 1)
+    top, leading = row_at < HALF, lane_at < HALF
+    as_sent = (top & (~leading | (row_at <= lane_at))) | (~top & ~leading & (row_at > lane_at))
+    on_corner = ~top & (row_at == lane_at)
+
+    def unfold(j):
+        x = folded_a[j]
+        x = jnp.concatenate([x, pltpu.roll(x, HALF, 1)], axis=0)
+        return jnp.where(on_corner, corner_a[pl.ds(j, 1), :], jnp.where(as_sent, x, x.T))
+
+    def take(j):
+        head(j).wait_recv()
+        head_pass(j).start()
+
+    def place_row(j):
+        q, r = j // 2, j % 2
+        head_pass(j).wait_recv()
+        for k in range(H + 1):
+            present = first_row + ROWS + j + k < total_rows
+            weight = jnp.where(present, jnp.float32(1.0), jnp.float32(0.0))
+            if k > 0:
+                weight = jnp.where(mask_a[pl.ds(k, 1), pl.ds(j, 1)] == 1, weight, jnp.float32(0.0))
+            x = masked(weight, ahead[j, k - 1] if k > 0 else unfold(j))
+            place_right(PAIRS + q, r, k, x)
+            if 0 < k < H - j:
+                place_right_t(PAIRS + q, r, k, x.T)
+
+    def add_terms(q):
         for pair in range(H // 2 + q, PAIRS):
             for c in range(PAIRS, PAIRS + q + H // 2 + 1):
                 d = c - pair
@@ -280,13 +327,29 @@
                 first = c >= PAIRS + H // 2 and q == c - PAIRS - H // 2
                 emit(pair, d, multiply(pair, d, at, at + 2), not first)
 
+    take(2)
+    fold_send.wait_recv()
+    fold_pass.start()
+    fold_pass.wait_recv()
+    place_row(0)
+    place_row(1)
+    take(3)
+    add_terms(0)
+    place_row(2)
+    take(4)
+    place_row(3)
+    add_terms(1)
+    take(5)
+    place_row(4)
+    place_row(5)
+
     for j in range(H):
         head(j).wait_send()
         tail(j).wait_send()
         head_pass(j).wait_send()
         tail_pass(j).wait_send()
-    mask_head.wait_send()
-    mask_tail.wait_send()
+    for copy in (mask_head, mask_tail, fold_send, fold_pass, corner_send):
+        copy.wait_send()
 
 
 def on_device(upper, block_mask, keep_mask):
@@ -302,32 +365,38 @@
         ),
         in_specs=[
             pl.BlockSpec(memory_space=pltpu.HBM),
-            pl.BlockSpec(memory_space=pltpu.SMEM),
-            pl.BlockSpec(memory_space=pltpu.VMEM),
-            pl.BlockSpec(memory_space=pltpu.SMEM),
+            pl.BlockSpec(memory_space=pltpu.HBM),
+            pl.BlockSpec(memory_space=pltpu.HBM),
         ],
         out_specs=[pl.BlockSpec(memory_space=pltpu.VMEM)] * 4,
         scratch_shapes=[
             pltpu.VMEM((ROWS, H + 1, B, B), f32),
             pltpu.VMEM((H, H, B, B), f32),
-            pltpu.VMEM((H, H + 1, B, B), f32),
+            pltpu.VMEM((H, H, B, B), f32),
             pltpu.VMEM((H + 1, ROWS), jnp.int32),
             pltpu.VMEM((H + 1, ROWS), jnp.int32),
-            pltpu.SemaphoreType.DMA,
+            pltpu.SMEM((H + 1, ROWS), jnp.int32),
+            pltpu.SMEM((ROWS, 2 * H + 1), jnp.int32),
+            pltpu.VMEM((H, B, B), f32),
+            pltpu.VMEM((H, HALF, B), f32),
+            pltpu.VMEM((8, B), f32),
+            pltpu.VMEM((H, HALF, B), f32),
+            pltpu.VMEM((8, B), f32),
+            pltpu.SemaphoreType.DMA((4,)),
             pltpu.SemaphoreType.DMA((2 * H,)),
             pltpu.SemaphoreType.DMA((2 * H,)),
             pltpu.SemaphoreType.DMA((2 * H,)),
             pltpu.SemaphoreType.DMA((2 * H,)),
-            pltpu.SemaphoreType.DMA((2,)),
-            pltpu.SemaphoreType.DMA((2,)),
+            pltpu.SemaphoreType.DMA((5,)),
+            pltpu.SemaphoreType.DMA((5,)),
             pltpu.SemaphoreType.REGULAR,
         ],
         compiler_params=pltpu.CompilerParams(
             collective_id=0, has_side_effects=True, vmem_limit_bytes=18 * 2**20
         ),
     )
-    masks = block_mask.T
-    parts = spread(upper, masks, masks, keep_mask)
+    held = [pltpu.with_memory_space_constraint(x, pltpu.HBM) for x in (upper, block_mask.T, keep_mask)]
+    parts = spread(*held)
     parts = [pltpu.with_memory_space_constraint(x, pltpu.VMEM) for x in parts]
     return pl.pallas_call(
         finish,

time: 57.6 us -> 47.2 us (0.82)
  Pallas kernels: 56 us -> 47.1 us
  local copies, waits for them, and re-layouts: 1.38 us -> 0.01 us
    pallas_call x1, Pallas kernels: 52.9 us -> 44 us  [on_device(): parts = spread(*held)]
    unnamed x4 -> x2, local copies, waits for them, and re-layouts: 1.38 us -> 0.01 us
where the time goes in v2:
time: 47.2 us; the launch traced here: 47.1 us
  Pallas kernels  47.1 us (100%)
    pallas_call x1, Pallas kernels, on_device(): parts = spread(*held)  44 us
    pallas_call x1, Pallas kernels, on_device(): pl.pallas_call(finish, out_shape=jax.ShapeDtypeStruct((ROWS, 2 * H + 1, H...  3.1 us

profile of v2, /device:TPU:1, one launch (start us, length us, event | category | flops | bytes accessed | tf_op | source)
XLA Modules:
  0.0 47.1 jit_solution(7739336530311480567)
XLA Ops:
  0.0 0.0 copy-start
  0.0 44.0 %shard_map.37 = (f32[12,13,64,128]{3,2,1,0:T(8,128)S(1)}, bf16[12,1792,256]{2,1,0:T(8,128)(2,1)S(1)}, bf16[12,1792,256]{2,1,0:T(8,128)(2,1)S(1)}, bf16[6,256,1792]{2,1,0:T(8,128)(2,1)S(1)}) custom-call(f32[12,7,128,128]{3,2,1,0:T(8,128)} %up.1, s32[7,12]{1,0:T(8,128)} %bitcast.1, s32[12,13]{1,0:T(8,128)} %keep_s.1), custom_call_target="tpu_custom_call" | custom-call | tf_op jit(solution)/shard_map/pallas_call | solution.py:399
  44.0 0.0 copy-done
  44.0 3.1 %shard_map.38 = f32[12,13,64,128]{3,2,1,0:T(8,128)} custom-call(f32[12,13,64,128]{3,2,1,0:T(8,128)S(1)} %get-tuple-element.9.out, bf16[12,1792,256]{2,1,0:T(8,128)(2,1)S(1)} %get-tuple-element.10.right_hi, bf16[12,1792,256]{2,1,0:T(8,128)(2,1)S(1)} %get-tuple-element.11.right_lo, bf16[6,256,1792]{2,1,0:T(8,128)(2,1)S(1)} %get-tuple-element.12.left, ...), custom_call_target="tpu_custom_call" | custom-call | tf_op jit(solution)/shard_map/pallas_call | solution.py:401
Async XLA Ops:
  0.0 44.0 %copy-start = (s32[12,13]{1,0:T(8,128)S(1)}, s32[12,13]{1,0:T(8,128)}, u32[]{:S(2)}) copy-start(s32[12,13]{1,0:T(8,128)} %keep_s.1) | copy-start | bytes 1876

commit v3 on v2

--- a/solution.py
+++ b/solution.py
@@ -49,7 +49,7 @@
     return jnp.where(kept, jnp.float32(1.0), jnp.float32(0.0))
 
 
-def finish(out, right_hi, right_lo, left, keep_s, final, tail, sem):
+def finish(out, right_hi, right_lo, left, keep, final, tail, keep_s, sem):
     n_part = lax.axis_size("row") * lax.axis_size("col")
     first_row = (lax.axis_index("row") * lax.axis_size("col") + lax.axis_index("col")) * ROWS
     last = PAIRS - 1
@@ -57,8 +57,11 @@
     copies = [pltpu.make_async_copy(out.at[pl.ds(2 * p, 2)], final.at[pl.ds(2 * p, 2)], sem.at[p]) for p in range(last)]
     copies.append(pltpu.make_async_copy(out.at[done, pl.ds(0, 2)], final.at[done, pl.ds(0, 2)], sem.at[last]))
     copies.append(pltpu.make_async_copy(out.at[done + 1, pl.ds(0, 1)], final.at[done + 1, pl.ds(0, 1)], sem.at[last + 1]))
+    load_keep = pltpu.make_async_copy(keep, keep_s, sem.at[last + 4])
+    load_keep.start()
     for copy in copies:
         copy.start()
+    load_keep.wait()
     for d in range(1, H + 1):
         at = WINDOW - 2 * d - 2
         total = window_product(left, right_hi, right_lo, last, d, at, at + 2)
@@ -272,9 +275,11 @@
     for a in range(H):
         tail(a).wait_recv()
         tail_pass(a).start()
-    for j in range(2):
+    for j in range(4):
         head(j).wait_recv()
         head_pass(j).start()
+    fold_send.wait_recv()
+    fold_pass.start()
     mask_tail.wait_recv()
     for a in range(H):
         tail_pass(a).wait_recv()
@@ -327,19 +332,15 @@
                 first = c >= PAIRS + H // 2 and q == c - PAIRS - H // 2
                 emit(pair, d, multiply(pair, d, at, at + 2), not first)
 
-    take(2)
-    fold_send.wait_recv()
-    fold_pass.start()
+    take(4)
+    take(5)
     fold_pass.wait_recv()
     place_row(0)
     place_row(1)
-    take(3)
     add_terms(0)
     place_row(2)
-    take(4)
     place_row(3)
     add_terms(1)
-    take(5)
     place_row(4)
     place_row(5)
 
@@ -401,14 +402,15 @@
     return pl.pallas_call(
         finish,
         out_shape=jax.ShapeDtypeStruct((ROWS, 2 * H + 1, HALF, B), f32),
-        in_specs=[pl.BlockSpec(memory_space=pltpu.VMEM)] * 4 + [pl.BlockSpec(memory_space=pltpu.SMEM)],
+        in_specs=[pl.BlockSpec(memory_space=pltpu.VMEM)] * 4 + [pl.BlockSpec(memory_space=pltpu.HBM)],
         out_specs=pl.BlockSpec(memory_space=pltpu.HBM),
         scratch_shapes=[
             pltpu.VMEM((2, 2 * H + 1, HALF, B), f32),
-            pltpu.SemaphoreType.DMA((PAIRS + 3,)),
+            pltpu.SMEM((ROWS, 2 * H + 1), jnp.int32),
+            pltpu.SemaphoreType.DMA((PAIRS + 4,)),
         ],
         compiler_params=pltpu.CompilerParams(vmem_limit_bytes=8 * 2**20),
-    )(*parts, keep_mask)
+    )(*parts, held[2])
 
 
 def solution(mesh):

time: 47.2 us -> 43.8 us (0.928)
  Pallas kernels: 47.1 us -> 43.7 us
    pallas_call x1, Pallas kernels: 44 us -> 41.3 us  [on_device(): parts = spread(*held)]
    pallas_call x1, Pallas kernels: 3.1 us -> 2.38 us  [on_device(): pl.pallas_call(finish, out_shape=jax.ShapeDtypeStruct((ROWS, 2 * H + 1, H...]
where the time goes in v3:
time: 43.8 us; the launch traced here: 43.7 us
  Pallas kernels  43.7 us (100%)
    pallas_call x1, Pallas kernels, on_device(): parts = spread(*held)  41.3 us
    pallas_call x1, Pallas kernels, on_device(): pl.pallas_call(finish, out_shape=jax.ShapeDtypeStruct((ROWS, 2 * H + 1, H...  2.38 us

profile of v3, /device:TPU:1, one launch (start us, length us, event | category | flops | bytes accessed | tf_op | source)
XLA Modules:
  0.0 43.7 jit_solution(7557038604094290434)
XLA Ops:
  0.0 41.3 %shard_map.37 = (f32[12,13,64,128]{3,2,1,0:T(8,128)S(1)}, bf16[12,1792,256]{2,1,0:T(8,128)(2,1)S(1)}, bf16[12,1792,256]{2,1,0:T(8,128)(2,1)S(1)}, bf16[6,256,1792]{2,1,0:T(8,128)(2,1)S(1)}) custom-call(f32[12,7,128,128]{3,2,1,0:T(8,128)} %up.1, s32[7,12]{1,0:T(8,128)} %bitcast.1, s32[12,13]{1,0:T(8,128)} %keep.3), custom_call_target="tpu_custom_call" | custom-call | tf_op jit(solution)/shard_map/pallas_call | solution.py:400
  41.3 2.4 %shard_map.38 = f32[12,13,64,128]{3,2,1,0:T(8,128)} custom-call(f32[12,13,64,128]{3,2,1,0:T(8,128)S(1)} %get-tuple-element.9.out, bf16[12,1792,256]{2,1,0:T(8,128)(2,1)S(1)} %get-tuple-element.10.right_hi, bf16[12,1792,256]{2,1,0:T(8,128)(2,1)S(1)} %get-tuple-element.11.right_lo, bf16[6,256,1792]{2,1,0:T(8,128)(2,1)S(1)} %get-tuple-element.12.left, ...), custom_call_target="tpu_custom_call" | custom-call | tf_op jit(solution)/shard_map/pallas_call | solution.py:402
